TPU v7x, 32 devices: a whole 2x2x4 slice. The times are simulated.
32 devices in a mesh: phase: 4 (over y, x), slab: 8 (over z, core).
Axes of the slice: x: 2, y: 2, z: 4, core: 2. Of those that a mesh axis runs over, the one named last changes fastest.
Arguments:
- pressure: float32 [2, 16, 32, 24576], P(None, 'phase', None, 'slab'), may hold values from -6 to 6
- mode_shapes: float32 [1024, 24576], P('phase', 'slab'), may hold values from -0.0546875 to 0.0546875
- point_weight: float32 [24576], P('slab'), may hold values from 0.5 to 2
- panel_order: int32 [8], replicated, may hold values from 0 to 7, each once
Outputs:
- influence: float32 [2, 16, 32, 1024], P(None, None, 'phase', 'slab')
Inputs may be any that keep to these rules, and one draw needn't show every extreme that they name: panel_order names each of 0 to 7 once.
All inputs are finite; a program needn't handle non-finite values.
Results may differ from a plain program's by a relative error of at most 0.00007.
Values sent between devices are 32-bit elements; how exact they have to be, the bound alone decides.
A program may use at most 64 MiB of HBM per device.

v0:
```python
import math

import jax
import jax.numpy as jnp
from jax import lax
from jax.sharding import PartitionSpec as P


def blade_table(blades, count):
    phases = jnp.arange(count, dtype=jnp.int32)
    target = jnp.arange(blades, dtype=jnp.int32)
    index = target[:, None] * phases[None, :] % blades
    theta = index.astype(jnp.float32) * (2.0 * math.pi / blades)
    cosine = jnp.cos(theta)
    sine = jnp.sin(theta)
    upper = jnp.concatenate([cosine, -sine], axis=1)
    lower = jnp.concatenate([sine, cosine], axis=1)
    return jnp.concatenate([upper, lower], axis=0) * (1.0 / math.sqrt(blades))


def shards(pressure, mode_shapes, point_weight, panel_order):
    weighted = mode_shapes * point_weight[None, :]
    phase_dev = pressure.shape[1]
    excite = pressure.shape[2]
    rows = pressure.reshape(2 * phase_dev * excite, pressure.shape[3])
    partial_forces = lax.dot_general(
        rows,
        lax.all_gather(weighted, "phase", axis=0, tiled=True),
        (((1,), (1,)), ((), ())),
        precision=lax.Precision.HIGHEST,
        preferred_element_type=jnp.float32,
    )
    row_count = partial_forces.shape[0]
    panel_count = panel_order.shape[0]
    panels = partial_forces.reshape(row_count, panel_count, -1)
    selector = (panel_order[:, None] == jnp.arange(panel_count, dtype=jnp.int32)[None, :]).astype(
        jnp.float32
    )
    reordered = jnp.einsum(
        "rqc,pq->rpc", panels, selector, precision=lax.Precision.HIGHEST
    ).reshape(row_count, -1)
    slab_count = lax.axis_size("slab")
    total = lax.psum(reordered, "slab")
    keep_width = total.shape[1] // slab_count
    share = lax.dynamic_slice_in_dim(total, lax.axis_index("slab") * keep_width, keep_width, 1)
    mode_local = share.shape[1]
    forces = share.reshape(2, phase_dev, excite, mode_local)
    blades = phase_dev * lax.axis_size("phase")
    gathered = lax.all_to_all(forces, "phase", split_axis=2, concat_axis=1, tiled=True)
    table = blade_table(blades, blades)
    result = jnp.dot(
        table,
        gathered.reshape(2 * blades, -1),
        precision=lax.Precision.HIGHEST,
        preferred_element_type=jnp.float32,
    )
    result = result.reshape(2, blades, -1, mode_local)
    return result


def solution(mesh):
    placed = (P(None, "phase", None, "slab"), P("phase", "slab"), P("slab"), P())
    return jax.shard_map(
        shards,
        mesh=mesh,
        in_specs=placed,
        out_specs=P(None, None, "phase", "slab"),
        check_vma=False,
    )
```

profile of v0, /device:TPU:0, one launch (start us, length us, event | category | flops | bytes accessed | tf_op | source)
XLA Modules:
  0.0 232.2 jit_solution(12579367385076534090)
XLA Ops:
  6.5 0.0 copy-start
  6.5 0.0 all-gather.2.cloned.1.call-start
  6.5 4.0 %broadcast_multiply_fusion = f32[256,3072]{1,0:T(8,128)} fusion(f32[256,3072]{1,0:T(8,128)} %param.5, f32[3072]{0:T(1024)} %param.6), kind=kLoop, calls=%fused_computation | loop fusion | flops 786432 | bytes 6303744 | tf_op jit(solution)/shard_map/mul | solution.py:22
  10.6 0.0 all-gather.2.cloned.1.call-update
  10.6 0.0 all-reduce.2.cloned.1.call-start
  10.6 125.3 %all-gather.2.cloned.1.call-done = f32[1024,3072]{1,0:T(8,128)} async-done(((f32[256,3072]{1,0:T(8,128)}), f32[1024,3072]{1,0:T(8,128)}) %all-gather.2.cloned.1.call-update) | async-done | bytes 12582928 | tf_op jit(solution)/shard_map/all_gather | solution.py:28
  136.0 0.0 copy-done
  136.0 0.0 copy-start.1
  136.0 13.5 %fusion.15 = f32[1024,256]{1,0:T(8,128)} fusion(f32[1024,3072]{1,0:T(8,128)} %all-gather.2.cloned.1.call-done, f32[256,3072]{1,0:T(8,128)S(1)} %bitcast.44), kind=kOutput, calls=%fused_computation.25 | convolution fusion | flops 9663676416 | bytes 16777216 | tf_op jit(solution)/shard_map/dot_general | solution.py:26
  149.5 2.5 %copy.19 = f32[256,8,128]{2,1,0:T(8,128)} copy(f32[256,8,128]{0,2,1:T(8,128)} %bitcast.45) | data formatting | bytes 2097152 | tf_op jit(solution)/shard_map/reshape | solution.py:35
  152.0 0.0 copy-done.1
  152.0 1.8 fusion.11
  153.9 1.2 copy.38
  155.1 0.0 all-reduce.2.cloned.1.call-update
  155.1 0.1 fusion.13
  155.2 0.1 fusion.8
  155.2 58.8 %all-reduce.2.cloned.1.call-done = f32[256,1024]{1,0:T(8,128)} async-done(((f32[256,1024]{1,0:T(8,128)}), f32[256,1024]{1,0:T(8,128)}) %all-reduce.2.cloned.1.call-update) | async-done | bytes 1048592 | tf_op jit(solution)/shard_map/psum | solution.py:43
  214.1 0.9 constant_dynamic-slice_fusion
  215.0 0.7 copy.20
  215.7 3.6 %all-to-all-start = ((f32[2,4,32,128]{3,1,0,2:T(4,128)}), f32[2,4,32,128]{3,1,0,2:T(4,128)S(1)}, u32[]{:S(2)}, u32[]{:S(2)}) async-start(f32[2,4,32,128]{3,1,0,2:T(4,128)} %copy.20), calls=%async_computation | async-start | bytes 262144 | tf_op jit(solution)/shard_map/all_to_all | solution.py:49
  219.3 0.1 maximum_multiply_fusion
  219.4 4.9 %all-to-all-done = f32[2,4,32,128]{3,1,0,2:T(4,128)S(1)} async-done(((f32[2,4,32,128]{3,1,0,2:T(4,128)}), f32[2,4,32,128]{3,1,0,2:T(4,128)S(1)}, u32[]{:S(2)}, u32[]{:S(2)}) %all-to-all-start) | async-done | bytes 131104 | tf_op jit(solution)/shard_map/all_to_all | solution.py:49
  224.4 0.3 fusion
  224.7 0.7 copy.24
  (2 shorter events, 0.0 us)
Async XLA Ops:
  6.5 129.4 %copy-start = (f32[2,4,32,3072]{3,2,1,0:T(8,128)S(1)}, f32[2,4,32,3072]{3,2,1,0:T(8,128)}, u32[]{:S(2)}) copy-start(f32[2,4,32,3072]{3,2,1,0:T(8,128)} %param.4) | copy-start | bytes 9437188
  6.5 129.4 %all-gather.2.cloned.1.call-start = ((), (), s32[]{:S(2)}) async-start(), calls=%async_computation.1 | async-start | bytes 15728640 | tf_op jit(solution)/shard_map/all_gather | solution.py:28
  10.6 203.5 %all-reduce.2.cloned.1.call-start = ((), (), s32[]{:S(2)}) async-start(), calls=%async_computation.2 | async-start | bytes 2097152 | tf_op jit(solution)/shard_map/psum | solution.py:43
  136.0 16.0 %copy-start.1 = (s32[8]{0:T(128)S(1)}, s32[8]{0:T(128)}, u32[]{:S(2)}) copy-start(s32[8]{0:T(128)} %param.7) | copy-start | bytes 100
  215.7 8.6 %all-to-all-start = ((f32[2,4,32,128]{3,1,0,2:T(4,128)}), f32[2,4,32,128]{3,1,0,2:T(4,128)S(1)}, u32[]{:S(2)}, u32[]{:S(2)}) async-start(f32[2,4,32,128]{3,1,0,2:T(4,128)} %copy.20), calls=%async_computation | async-start | bytes 262144 | tf_op jit(solution)/shard_map/all_to_all | solution.py:49
Sparse Core Ops, SparseCore 0:
  10.7 125.2 all-gather.1
  155.2 58.7 all-reduce.1
where the time goes:
time: 233 us; the launch traced here: 232 us
  waiting for transfers between devices  189 us (81%)
  matrix products  15.6 us (7%)
  between operations  13.4 us (6%)
  local copies, waits for them, and re-layouts  6.15 us (3%)
  other arithmetic  4.23 us (2%)
  starting transfers between devices  3.66 us (2%)
    all_gather x1, waiting for transfers between devices, shards(): lax.all_gather(weighted, 'phase', axis=0, tiled=True)  125 us
    psum x1, waiting for transfers between devices, shards(): total = lax.psum(reordered, 'slab')  58.8 us
    dot_general x1, matrix products, shards(): lax.dot_general(rows, lax.all_gather(weighted, 'phase', axis=0, tiled=Tru...  13.5 us
    all_to_all x1, waiting for transfers between devices, shards(): lax.all_to_all(forces, 'phase', split_axis=2, concat_axis=1, tiled=True)  4.94 us
  transfers between devices with their start and end apart: 3, of which 3 were waited for; matrix products, arithmetic and copies ran while one was open for 0% of the time, Pallas kernels for 0%

commit v1 on v0

--- a/solution.py
+++ b/solution.py
@@ -3,7 +3,16 @@
 import jax
 import jax.numpy as jnp
 from jax import lax
+from jax.experimental import pallas as pl
+from jax.experimental.pallas import tpu as pltpu
 from jax.sharding import PartitionSpec as P
+
+MESH = pl.DeviceIdType.MESH
+F32 = jnp.float32
+BF16 = jnp.bfloat16
+SLABS = 8
+CHUNKS = 4
+OWN, REM = 0, 1
 
 
 def blade_table(blades, count):
@@ -18,7 +27,7 @@
     return jnp.concatenate([upper, lower], axis=0) * (1.0 / math.sqrt(blades))
 
 
-def shards(pressure, mode_shapes, point_weight, panel_order):
+def general(pressure, mode_shapes, point_weight, panel_order):
     weighted = mode_shapes * point_weight[None, :]
     phase_dev = pressure.shape[1]
     excite = pressure.shape[2]
@@ -58,7 +67,285 @@
     return result
 
 
+def split(value):
+    high = value.astype(BF16)
+    return high, (value - high.astype(F32)).astype(BF16)
+
+
+def product(a_high, a_low, b_high, b_low):
+    def dot(a, b):
+        return lax.dot_general(a, b, (((1,), (1,)), ((), ())), preferred_element_type=F32)
+
+    return dot(a_high, b_high) + dot(a_high, b_low) + dot(a_low, b_high)
+
+
+PIECES = {
+    OWN: ((0, 2, 0, 4), (2, 1, 0, 4), (3, 1, 0, 4)),
+    REM: ((0, 3, 0, 2), (0, 3, 2, 1), (0, 3, 3, 1), (3, 1, 0, 4)),
+}
+
+
+def kernel(
+    index_ref, a_hbm, b_hbm, w_ref, out_ref,
+    a_own, b_own, a_rem, b_rem, a_hi, a_lo, b_hi, b_lo, part, parts, red, plane, picked, gathered,
+    load_sem, a_send, a_recv, b_send, b_recv, r_send, r_recv, p_send, p_recv, g_send, g_recv,
+):
+    p = lax.axis_index("phase")
+    d = lax.axis_index("slab")
+    x, y = p % 2, p // 2
+    x_near = y * 2 + (1 - x)
+    y_near = (1 - y) * 2 + x
+
+    loads = [
+        pltpu.make_async_copy(a_hbm.at[:, :, pl.ds(8 * g, 8), :], a_own.at[g], load_sem.at[g])
+        for g in range(CHUNKS)
+    ]
+    loads.append(pltpu.make_async_copy(b_hbm, b_own, load_sem.at[CHUNKS]))
+    for load in loads:
+        load.start()
+
+    barrier = pltpu.get_barrier_semaphore()
+    for o in range(1, 4):
+        pl.semaphore_signal(
+            barrier, inc=1, device_id={"phase": (p + o) % 4, "slab": d}, device_id_type=MESH
+        )
+    for o in range(1, SLABS):
+        pl.semaphore_signal(
+            barrier, inc=1, device_id={"phase": p, "slab": (d + o) % SLABS}, device_id_type=MESH
+        )
+    pl.semaphore_wait(barrier, 3 + SLABS - 1)
+
+    def a_copy(t):
+        return pltpu.make_async_remote_copy(
+            src_ref=a_hbm.at[:, :, pl.ds(8 * t, 8), :], dst_ref=a_rem.at[t],
+            send_sem=a_send.at[t], recv_sem=a_recv.at[t],
+            device_id={"phase": x_near, "slab": d}, device_id_type=MESH,
+        )
+
+    def b_copy(t):
+        return pltpu.make_async_remote_copy(
+            src_ref=b_hbm.at[pl.ds(64 * t, 64)], dst_ref=b_rem.at[pl.ds(64 * t, 64)],
+            send_sem=b_send.at[t], recv_sem=b_recv.at[t],
+            device_id={"phase": y_near, "slab": d}, device_id_type=MESH,
+        )
+
+    def piece(kind, i, kk, act):
+        slot, slots, group, groups = PIECES[kind][i]
+        peer = ((kind + x) % 2) * 4 + kk
+        where = (pl.ds(slot, slots), pl.ds(group, groups))
+
+        @pl.when(peer != d)
+        def _():
+            act(pltpu.make_async_remote_copy(
+                src_ref=part.at[(kind * 4 + kk,) + where], dst_ref=parts.at[(d,) + where],
+                send_sem=r_send.at[i, kind * 4 + kk], recv_sem=r_recv.at[i, d],
+                device_id={"phase": p, "slab": peer}, device_id_type=MESH,
+            ))
+
+    def send(kind, i):
+        for kk in range(4):
+            piece(kind, i, kk, lambda copy: copy.start())
+
+    def split_a(source, g, kind):
+        high, low = split(source[g].reshape(64, -1))
+        rows = pl.ds(kind * 256 + 64 * g, 64)
+        a_hi[rows], a_lo[rows] = high, low
+
+    def split_b(source, t, kind):
+        high, low = split(source[pl.ds(64 * t, 64)] * w_ref[...])
+        rows = pl.ds(kind * 256 + 64 * t, 64)
+        b_hi[rows], b_lo[rows] = high, low
+
+    def block(kind, group, groups, slot, slots):
+        rows = pl.ds(kind * 256 + 64 * group, 64 * groups)
+        cols = pl.ds(128 * slot, 128 * slots)
+        value = product(a_hi[rows], a_lo[rows], b_hi[cols], b_lo[cols])
+        value = value.reshape(groups, 2, 4, 8, 128 * slots)
+        for kk in range(4):
+            for s in range(slots):
+                part[kind * 4 + kk, slot + s, pl.ds(group, groups)] = (
+                    value[:, :, kk, :, 128 * s:128 * (s + 1)]
+                )
+
+    for t in range(2):
+        a_copy(t).start()
+        b_copy(t).start()
+
+    for load in loads:
+        load.wait()
+    for t in range(CHUNKS):
+        split_a(a_own, t, OWN)
+        split_b(b_own, t, OWN)
+    block(OWN, 0, 4, 0, 2)
+    send(OWN, 0)
+
+    for t in range(CHUNKS):
+        a_copy(t).wait()
+        if t + 2 < CHUNKS:
+            a_copy(t + 2).start()
+        b_copy(t).wait()
+        if t + 2 < CHUNKS:
+            b_copy(t + 2).start()
+        split_a(a_rem, t, REM)
+        split_b(b_rem, t, REM)
+        if t == 1:
+            block(REM, 0, 2, 0, 3)
+            send(REM, 0)
+            block(OWN, 0, 4, 2, 1)
+            send(OWN, 1)
+        if t == 2:
+            block(REM, 2, 1, 0, 3)
+            send(REM, 1)
+        if t == 3:
+            block(REM, 3, 1, 0, 3)
+            send(REM, 2)
+            block(REM, 0, 4, 3, 1)
+            send(REM, 3)
+            block(OWN, 0, 4, 3, 1)
+            send(OWN, 2)
+
+    mine = (d // 4 + x) % 2
+    for kind in (OWN, REM):
+        @pl.when(mine == kind)
+        def _():
+            for i, (slot, slots, group, groups) in enumerate(PIECES[kind]):
+                for o in range(1, SLABS):
+                    other = (d + o) % SLABS
+                    landed = parts.at[other, pl.ds(slot, slots), pl.ds(group, groups)]
+                    pltpu.make_async_copy(landed, landed, r_recv.at[i, other]).wait()
+
+    total = part[mine * 4 + d % 4]
+    for o in range(1, SLABS):
+        total = total + parts[(d + o) % SLABS]
+    red[...] = total
+
+    def plane_copy(o):
+        peer = (p + o) % 4
+        return pltpu.make_async_remote_copy(
+            src_ref=red.at[:, peer], dst_ref=plane.at[pl.ds(4 * p, 4)],
+            send_sem=p_send.at[o], recv_sem=p_recv.at[p],
+            device_id={"phase": peer, "slab": d}, device_id_type=MESH,
+        )
+
+    for o in range(1, 4):
+        plane_copy(o).start()
+    plane[pl.ds(4 * p, 4)] = red[:, p]
+    for o in range(1, 4):
+        other = (p + o) % 4
+        landed = plane.at[pl.ds(4 * other, 4)]
+        pltpu.make_async_copy(landed, landed, p_recv.at[other]).wait()
+
+    def slab_copy(o):
+        peer = (d + o) % SLABS
+        return pltpu.make_async_remote_copy(
+            src_ref=picked.at[o], dst_ref=gathered.at[d],
+            send_sem=g_send.at[o], recv_sem=g_recv.at[d],
+            device_id={"phase": p, "slab": peer}, device_id_type=MESH,
+        )
+
+    for o in range(1, SLABS):
+        peer = (d + o) % SLABS
+        for half in range(2):
+            picked[o, half] = plane[index_ref[half * SLABS + peer]]
+        slab_copy(o).start()
+    for half in range(2):
+        gathered[d, half] = plane[index_ref[half * SLABS + d]]
+    for o in range(1, SLABS):
+        other = (d + o) % SLABS
+        landed = gathered.at[other]
+        pltpu.make_async_copy(landed, landed, g_recv.at[other]).wait()
+
+    blades = 16
+    scale = 1.0 / math.sqrt(blades)
+    cosine = [round(math.cos(2 * math.pi * i / blades), 15) * scale for i in range(blades)]
+    sine = [round(math.sin(2 * math.pi * i / blades), 15) * scale for i in range(blades)]
+    for b in range(blades):
+        real, imag = None, None
+        for k in range(blades):
+            c, s = cosine[k * b % blades], sine[k * b % blades]
+            re, im = gathered[k % 8, k // 8, 0], gathered[k % 8, k // 8, 1]
+            for sign, coef, u, v in ((-1.0, c, re, im), (1.0, s, im, re)):
+                if coef == 0.0:
+                    continue
+                first = u * (coef if sign < 0 else -coef)
+                second = v * coef
+                real = first if real is None else real + first
+                imag = second if imag is None else imag + second
+        out_ref[0, b] = real
+        out_ref[1, b] = imag
+
+    for kind in (OWN, REM):
+        for i in range(len(PIECES[kind])):
+            for kk in range(4):
+                piece(kind, i, kk, lambda copy: copy.wait_send())
+    for o in range(1, 4):
+        plane_copy(o).wait_send()
+    for o in range(1, SLABS):
+        slab_copy(o).wait_send()
+
+
+def fused(pressure, mode_shapes, point_weight, panel_order):
+    points = pressure.shape[3]
+    owner = panel_order // 2
+    half = jnp.arange(2, dtype=jnp.int32)[:, None]
+    far = (owner[None, :] // 2 != half).astype(jnp.int32)
+    index = ((half * 2 + owner[None, :] % 2) * 4 + far * 2 + panel_order[None, :] % 2).reshape(-1)
+    vmem = pltpu.VMEM
+    dma = pltpu.SemaphoreType.DMA
+    return pl.pallas_call(
+        kernel,
+        out_shape=jax.ShapeDtypeStruct((2, 16, 8, 128), F32),
+        in_specs=[
+            pl.BlockSpec(memory_space=pltpu.SMEM),
+            pl.BlockSpec(memory_space=pl.ANY),
+            pl.BlockSpec(memory_space=pl.ANY),
+            pl.BlockSpec(memory_space=pltpu.VMEM),
+        ],
+        out_specs=pl.BlockSpec(memory_space=pltpu.VMEM),
+        scratch_shapes=[
+            vmem((4, 2, 4, 8, points), F32),
+            vmem((256, points), F32),
+            vmem((4, 2, 4, 8, points), F32),
+            vmem((256, points), F32),
+            vmem((512, points), BF16),
+            vmem((512, points), BF16),
+            vmem((512, points), BF16),
+            vmem((512, points), BF16),
+            vmem((8, 4, 4, 2, 8, 128), F32),
+            vmem((8, 4, 4, 2, 8, 128), F32),
+            vmem((4, 4, 2, 8, 128), F32),
+            vmem((16, 2, 8, 128), F32),
+            vmem((8, 2, 2, 8, 128), F32),
+            vmem((8, 2, 2, 8, 128), F32),
+            dma((5,)),
+            dma((4,)), dma((4,)), dma((4,)), dma((4,)),
+            dma((4, 8)), dma((4, 8)),
+            dma((4,)), dma((4,)),
+            dma((8,)), dma((8,)),
+        ],
+        compiler_params=pltpu.CompilerParams(
+            collective_id=0, has_side_effects=True, vmem_limit_bytes=56 * 1024 * 1024
+        ),
+        cost_estimate=pl.CostEstimate(
+            flops=6 * 512 * 512 * points, bytes_accessed=16 * 256 * points, transcendentals=0
+        ),
+    )(index, pressure, mode_shapes, point_weight.reshape(1, points))
+
+
 def solution(mesh):
+    def shards(pressure, mode_shapes, point_weight, panel_order):
+        fits = (
+            mesh.shape["phase"] == 4
+            and mesh.shape["slab"] == SLABS
+            and pressure.shape[:3] == (2, 4, 32)
+            and pressure.shape[3] % 256 == 0
+            and pressure.shape[3] <= 3072
+            and mode_shapes.shape[0] == 256
+            and panel_order.shape[0] == 8
+        )
+        body = fused if fits else general
+        return body(pressure, mode_shapes, point_weight, panel_order)
+
     placed = (P(None, "phase", None, "slab"), P("phase", "slab"), P("slab"), P())
     return jax.shard_map(
         shards,

time: 233 us -> 105 us (0.45)
  waiting for transfers between devices: 189 us -> 0 us
  Pallas kernels: 0 us -> 102 us
  matrix products: 15.6 us -> 0 us
  between operations: 13.4 us -> 0.02 us
  local copies, waits for them, and re-layouts: 6.15 us -> 2.16 us
  starting transfers between devices: 3.66 us -> 0 us
  other arithmetic: 4.23 us -> 0.76 us
    all_gather x1 -> x0, waiting for transfers between devices: 125 us -> none  [shards(): lax.all_gather(weighted, 'phase', axis=0, tiled=True)]
    pallas_call x0 -> x1, Pallas kernels: none -> 102 us  [fused(): pl.pallas_call(kernel, out_shape=jax.ShapeDtypeStruct((2, 16, 8, 128), F3...]
    psum x1 -> x0, waiting for transfers between devices: 58.8 us -> none  [shards(): total = lax.psum(reordered, 'slab')]
    dot_general x3 -> x0, matrix products: 15.6 us -> none  [the longest x1 13.5 us: shards(): lax.dot_general(rows, lax.all_gather(weighted, 'phase', axis=0, tiled=Tru...]
    all_to_all x1 -> x0, waiting for transfers between devices: 4.94 us -> none  [shards(): lax.all_to_all(forces, 'phase', split_axis=2, concat_axis=1, tiled=True)]
    mul x2 -> x1, other arithmetic: 4.11 us -> 0.01 us  [fused(): half * 2 + owner[None, :] % 2]
    all_to_all x1 -> x0, starting transfers between devices: 3.62 us -> none  [shards(): lax.all_to_all(forces, 'phase', split_axis=2, concat_axis=1, tiled=True)]
    reshape x2 -> x0, local copies, waits for them, and re-layouts: 3.27 us -> none  [the longest x1 2.53 us: shards(): panels = partial_forces.reshape(row_count, panel_count, -1)]
  transfers between devices with their start and end apart: 3 -> 0, of which waited for: 3 -> 0; matrix products, arithmetic and copies ran while one was open for 0% -> 0% of each run, Pallas kernels for 0% -> 0%
where the time goes in v1:
time: 105 us; the launch traced here: 104 us
  Pallas kernels  102 us (97%)
  local copies, waits for them, and re-layouts  2.16 us (2%)
    pallas_call x1, Pallas kernels, fused(): pl.pallas_call(kernel, out_shape=jax.ShapeDtypeStruct((2, 16, 8, 128), F3...  102 us

profile of v1, /device:TPU:0, one launch (start us, length us, event | category | flops | bytes accessed | tf_op | source)
XLA Modules:
  0.0 104.5 jit_solution(6522821539433160195)
XLA Ops:
  0.0 0.7 and_select_fusion.2
  0.7 0.1 fusion.1
  0.8 0.6 add.55.index_ref
  1.4 101.5 %shard_map.46 = f32[2,16,8,128]{3,2,1,0:T(8,128)} custom-call(s32[16]{0:T(128)} %add.55.index_ref, f32[2,4,32,3072]{3,2,1,0:T(8,128)} %a_hbm.1, f32[256,3072]{1,0:T(8,128)} %b_hbm.1, f32[1,3072]{1,0:T(1,128)} %bitcast.1), custom_call_target="tpu_custom_call" | custom-call | flops 4831838208 | bytes 12582912 | tf_op jit(solution)/shard_map/pallas_call | solution.py:295
  102.9 1.6 %copy.6 = f32[2,16,8,128]{3,2,1,0:T(8,128)} copy(f32[2,16,8,128]{3,2,1,0:T(8,128)} %shard_map.46) | data formatting | bytes 262144
  (2 shorter events, 0.0 us)

commit v2 on v1

--- a/solution.py
+++ b/solution.py
@@ -11,7 +11,8 @@
 F32 = jnp.float32
 BF16 = jnp.bfloat16
 SLABS = 8
-CHUNKS = 4
+CHUNKS = 8
+DEPTH = 3
 OWN, REM = 0, 1
 
 
@@ -86,88 +87,107 @@
 
 
 def kernel(
-    index_ref, a_hbm, b_hbm, w_ref, out_ref,
-    a_own, b_own, a_rem, b_rem, a_hi, a_lo, b_hi, b_lo, part, parts, red, plane, picked, gathered,
-    load_sem, a_send, a_recv, b_send, b_recv, r_send, r_recv, p_send, p_recv, g_send, g_recv,
+    order_ref, a_hbm, b_hbm, w_ref, out_ref,
+    a_own, b_own, a_rem, b_rem, a_hi, a_lo, b_hi, b_lo, part, sibling, chip, parts, red, plane, picked,
+    gathered,
+    load_sem, a_send, a_recv, b_send, b_recv, s_send, s_recv, r_send, r_recv, p_send, p_recv, g_send,
+    g_recv,
 ):
     p = lax.axis_index("phase")
     d = lax.axis_index("slab")
     x, y = p % 2, p // 2
+    z, core = d // 2, d % 2
     x_near = y * 2 + (1 - x)
     y_near = (1 - y) * 2 + x
-
-    loads = [
-        pltpu.make_async_copy(a_hbm.at[:, :, pl.ds(8 * g, 8), :], a_own.at[g], load_sem.at[g])
-        for g in range(CHUNKS)
-    ]
+    core_near = z * 2 + (1 - core)
+
+    barrier = pltpu.get_barrier_semaphore()
+    for o in range(1, 4):
+        pl.semaphore_signal(
+            barrier, inc=1, device_id={"phase": (p + o) % 4, "slab": d}, device_id_type=MESH
+        )
+    for o in range(1, SLABS):
+        pl.semaphore_signal(
+            barrier, inc=1, device_id={"phase": p, "slab": (d + o) % SLABS}, device_id_type=MESH
+        )
+
+    def a_chunk(t):
+        return a_hbm.at[t % 2, :, pl.ds(8 * (t // 2), 8), :]
+
+    loads = [pltpu.make_async_copy(a_chunk(t), a_own.at[t], load_sem.at[t]) for t in range(CHUNKS)]
     loads.append(pltpu.make_async_copy(b_hbm, b_own, load_sem.at[CHUNKS]))
     for load in loads:
         load.start()
-
-    barrier = pltpu.get_barrier_semaphore()
-    for o in range(1, 4):
-        pl.semaphore_signal(
-            barrier, inc=1, device_id={"phase": (p + o) % 4, "slab": d}, device_id_type=MESH
-        )
-    for o in range(1, SLABS):
-        pl.semaphore_signal(
-            barrier, inc=1, device_id={"phase": p, "slab": (d + o) % SLABS}, device_id_type=MESH
-        )
     pl.semaphore_wait(barrier, 3 + SLABS - 1)
 
     def a_copy(t):
         return pltpu.make_async_remote_copy(
-            src_ref=a_hbm.at[:, :, pl.ds(8 * t, 8), :], dst_ref=a_rem.at[t],
+            src_ref=a_chunk(t), dst_ref=a_rem.at[t],
             send_sem=a_send.at[t], recv_sem=a_recv.at[t],
             device_id={"phase": x_near, "slab": d}, device_id_type=MESH,
         )
 
     def b_copy(t):
         return pltpu.make_async_remote_copy(
-            src_ref=b_hbm.at[pl.ds(64 * t, 64)], dst_ref=b_rem.at[pl.ds(64 * t, 64)],
+            src_ref=b_hbm.at[pl.ds(32 * t, 32)], dst_ref=b_rem.at[pl.ds(32 * t, 32)],
             send_sem=b_send.at[t], recv_sem=b_recv.at[t],
             device_id={"phase": y_near, "slab": d}, device_id_type=MESH,
         )
 
-    def piece(kind, i, kk, act):
+    def core_copy(kind, i):
         slot, slots, group, groups = PIECES[kind][i]
-        peer = ((kind + x) % 2) * 4 + kk
+        where = (slice(None), pl.ds(slot, slots), pl.ds(group, groups))
+        return pltpu.make_async_remote_copy(
+            src_ref=part.at[(kind, 1 - core) + where], dst_ref=sibling.at[(kind,) + where],
+            send_sem=s_send.at[kind, i], recv_sem=s_recv.at[kind, i],
+            device_id={"phase": p, "slab": core_near}, device_id_type=MESH,
+        )
+
+    def peer_copy(kind, i, h, act):
+        slot, slots, group, groups = PIECES[kind][i]
+        peer_z = ((kind + x) % 2) * 2 + h
         where = (pl.ds(slot, slots), pl.ds(group, groups))
 
-        @pl.when(peer != d)
+        @pl.when(peer_z != z)
         def _():
             act(pltpu.make_async_remote_copy(
-                src_ref=part.at[(kind * 4 + kk,) + where], dst_ref=parts.at[(d,) + where],
-                send_sem=r_send.at[i, kind * 4 + kk], recv_sem=r_recv.at[i, d],
-                device_id={"phase": p, "slab": peer}, device_id_type=MESH,
+                src_ref=chip.at[(kind, h) + where], dst_ref=parts.at[(z,) + where],
+                send_sem=r_send.at[kind, i, h], recv_sem=r_recv.at[i, z],
+                device_id={"phase": p, "slab": peer_z * 2 + core}, device_id_type=MESH,
             ))
 
-    def send(kind, i):
-        for kk in range(4):
-            piece(kind, i, kk, lambda copy: copy.start())
-
-    def split_a(source, g, kind):
-        high, low = split(source[g].reshape(64, -1))
-        rows = pl.ds(kind * 256 + 64 * g, 64)
+    def forward(kind, i):
+        core_copy(kind, i).wait()
+        slot, slots, group, groups = PIECES[kind][i]
+        for h in range(2):
+            where = (h, pl.ds(slot, slots), pl.ds(group, groups))
+            chip[(kind,) + where] = part[(kind, core) + where] + sibling[(kind,) + where]
+            peer_copy(kind, i, h, lambda copy: copy.start())
+
+    def split_a(source, t, kind):
+        high, low = split(source[t].reshape(32, -1))
+        rows = pl.ds(kind * 256 + 32 * t, 32)
         a_hi[rows], a_lo[rows] = high, low
 
     def split_b(source, t, kind):
-        high, low = split(source[pl.ds(64 * t, 64)] * w_ref[...])
-        rows = pl.ds(kind * 256 + 64 * t, 64)
+        high, low = split(source[pl.ds(32 * t, 32)] * w_ref[...])
+        rows = pl.ds(kind * 256 + 32 * t, 32)
         b_hi[rows], b_lo[rows] = high, low
 
-    def block(kind, group, groups, slot, slots):
+    def block(kind, i):
+        slot, slots, group, groups = PIECES[kind][i]
         rows = pl.ds(kind * 256 + 64 * group, 64 * groups)
         cols = pl.ds(128 * slot, 128 * slots)
         value = product(a_hi[rows], a_lo[rows], b_hi[cols], b_lo[cols])
         value = value.reshape(groups, 2, 4, 8, 128 * slots)
         for kk in range(4):
             for s in range(slots):
-                part[kind * 4 + kk, slot + s, pl.ds(group, groups)] = (
+                part[kind, kk % 2, kk // 2, slot + s, pl.ds(group, groups)] = (
                     value[:, :, kk, :, 128 * s:128 * (s + 1)]
                 )
-
-    for t in range(2):
+        core_copy(kind, i).start()
+
+    for t in range(DEPTH):
         a_copy(t).start()
         b_copy(t).start()
 
@@ -176,47 +196,51 @@
     for t in range(CHUNKS):
         split_a(a_own, t, OWN)
         split_b(b_own, t, OWN)
-    block(OWN, 0, 4, 0, 2)
-    send(OWN, 0)
+    block(OWN, 0)
 
     for t in range(CHUNKS):
+        b_copy(t).wait()
+        if t + DEPTH < CHUNKS:
+            b_copy(t + DEPTH).start()
+        split_b(b_rem, t, REM)
+        if t == 7:
+            block(OWN, 2)
         a_copy(t).wait()
-        if t + 2 < CHUNKS:
-            a_copy(t + 2).start()
-        b_copy(t).wait()
-        if t + 2 < CHUNKS:
-            b_copy(t + 2).start()
+        if t + DEPTH < CHUNKS:
+            a_copy(t + DEPTH).start()
         split_a(a_rem, t, REM)
-        split_b(b_rem, t, REM)
-        if t == 1:
-            block(REM, 0, 2, 0, 3)
-            send(REM, 0)
-            block(OWN, 0, 4, 2, 1)
-            send(OWN, 1)
-        if t == 2:
-            block(REM, 2, 1, 0, 3)
-            send(REM, 1)
+        if t == 0:
+            forward(OWN, 0)
         if t == 3:
-            block(REM, 3, 1, 0, 3)
-            send(REM, 2)
-            block(REM, 0, 4, 3, 1)
-            send(REM, 3)
-            block(OWN, 0, 4, 3, 1)
-            send(OWN, 2)
+            block(REM, 0)
+            block(OWN, 1)
+        if t == 4:
+            forward(REM, 0)
+            forward(OWN, 1)
+        if t == 5:
+            block(REM, 1)
+        if t == 6:
+            forward(REM, 1)
+        if t == 7:
+            block(REM, 3)
+            forward(OWN, 2)
+            block(REM, 2)
+            forward(REM, 3)
+            forward(REM, 2)
 
     mine = (d // 4 + x) % 2
     for kind in (OWN, REM):
         @pl.when(mine == kind)
         def _():
             for i, (slot, slots, group, groups) in enumerate(PIECES[kind]):
-                for o in range(1, SLABS):
-                    other = (d + o) % SLABS
+                for o in range(1, 4):
+                    other = (z + o) % 4
                     landed = parts.at[other, pl.ds(slot, slots), pl.ds(group, groups)]
                     pltpu.make_async_copy(landed, landed, r_recv.at[i, other]).wait()
 
-    total = part[mine * 4 + d % 4]
-    for o in range(1, SLABS):
-        total = total + parts[(d + o) % SLABS]
+    total = chip[mine, z % 2]
+    for o in range(1, 4):
+        total = total + parts[(z + o) % 4]
     red[...] = total
 
     def plane_copy(o):
@@ -235,6 +259,11 @@
         landed = plane.at[pl.ds(4 * other, 4)]
         pltpu.make_async_copy(landed, landed, p_recv.at[other]).wait()
 
+    def panel(half, peer):
+        q = order_ref[peer]
+        off = q // 4 - half
+        return plane[(half * 2 + q // 2 % 2) * 4 + off * off * 2 + q % 2]
+
     def slab_copy(o):
         peer = (d + o) % SLABS
         return pltpu.make_async_remote_copy(
@@ -244,12 +273,11 @@
         )
 
     for o in range(1, SLABS):
-        peer = (d + o) % SLABS
         for half in range(2):
-            picked[o, half] = plane[index_ref[half * SLABS + peer]]
+            picked[o, half] = panel(half, (d + o) % SLABS)
         slab_copy(o).start()
     for half in range(2):
-        gathered[d, half] = plane[index_ref[half * SLABS + d]]
+        gathered[d, half] = panel(half, d)
     for o in range(1, SLABS):
         other = (d + o) % SLABS
         landed = gathered.at[other]
@@ -264,11 +292,10 @@
         for k in range(blades):
             c, s = cosine[k * b % blades], sine[k * b % blades]
             re, im = gathered[k % 8, k // 8, 0], gathered[k % 8, k // 8, 1]
-            for sign, coef, u, v in ((-1.0, c, re, im), (1.0, s, im, re)):
-                if coef == 0.0:
-                    continue
-                first = u * (coef if sign < 0 else -coef)
-                second = v * coef
+            terms = [(re * c, im * c)] if c else []
+            if s:
+                terms.append((im * -s, re * s))
+            for first, second in terms:
                 real = first if real is None else real + first
                 imag = second if imag is None else imag + second
         out_ref[0, b] = real
@@ -276,8 +303,8 @@
 
     for kind in (OWN, REM):
         for i in range(len(PIECES[kind])):
-            for kk in range(4):
-                piece(kind, i, kk, lambda copy: copy.wait_send())
+            for h in range(2):
+                peer_copy(kind, i, h, lambda copy: copy.wait_send())
     for o in range(1, 4):
         plane_copy(o).wait_send()
     for o in range(1, SLABS):
@@ -286,10 +313,6 @@
 
 def fused(pressure, mode_shapes, point_weight, panel_order):
     points = pressure.shape[3]
-    owner = panel_order // 2
-    half = jnp.arange(2, dtype=jnp.int32)[:, None]
-    far = (owner[None, :] // 2 != half).astype(jnp.int32)
-    index = ((half * 2 + owner[None, :] % 2) * 4 + far * 2 + panel_order[None, :] % 2).reshape(-1)
     vmem = pltpu.VMEM
     dma = pltpu.SemaphoreType.DMA
     return pl.pallas_call(
@@ -303,23 +326,26 @@
         ],
         out_specs=pl.BlockSpec(memory_space=pltpu.VMEM),
         scratch_shapes=[
-            vmem((4, 2, 4, 8, points), F32),
+            vmem((CHUNKS, 4, 8, points), F32),
             vmem((256, points), F32),
-            vmem((4, 2, 4, 8, points), F32),
+            vmem((CHUNKS, 4, 8, points), F32),
             vmem((256, points), F32),
             vmem((512, points), BF16),
             vmem((512, points), BF16),
             vmem((512, points), BF16),
             vmem((512, points), BF16),
-            vmem((8, 4, 4, 2, 8, 128), F32),
-            vmem((8, 4, 4, 2, 8, 128), F32),
+            vmem((2, 2, 2, 4, 4, 2, 8, 128), F32),
+            vmem((2, 2, 4, 4, 2, 8, 128), F32),
+            vmem((2, 2, 4, 4, 2, 8, 128), F32),
+            vmem((4, 4, 4, 2, 8, 128), F32),
             vmem((4, 4, 2, 8, 128), F32),
             vmem((16, 2, 8, 128), F32),
             vmem((8, 2, 2, 8, 128), F32),
             vmem((8, 2, 2, 8, 128), F32),
-            dma((5,)),
-            dma((4,)), dma((4,)), dma((4,)), dma((4,)),
-            dma((4, 8)), dma((4, 8)),
+            dma((CHUNKS + 1,)),
+            dma((CHUNKS,)), dma((CHUNKS,)), dma((CHUNKS,)), dma((CHUNKS,)),
+            dma((2, 4)), dma((2, 4)),
+            dma((2, 4, 2)), dma((4, 4)),
             dma((4,)), dma((4,)),
             dma((8,)), dma((8,)),
         ],
@@ -329,7 +355,7 @@
         cost_estimate=pl.CostEstimate(
             flops=6 * 512 * 512 * points, bytes_accessed=16 * 256 * points, transcendentals=0
         ),
-    )(index, pressure, mode_shapes, point_weight.reshape(1, points))
+    )(panel_order, pressure, mode_shapes, point_weight.reshape(1, points))
 
 
 def solution(mesh):

time: 105 us -> 101 us (0.962)
  Pallas kernels: 102 us -> 99.5 us
    pallas_call x1, Pallas kernels: 102 us -> 99.5 us  [fused(): pl.pallas_call(kernel, out_shape=jax.ShapeDtypeStruct((2, 16, 8, 128), F3...]
where the time goes in v2:
time: 101 us
  Pallas kernels  99.5 us (99%)
  local copies, waits for them, and re-layouts  1.57 us (2%)
    pallas_call x1, Pallas kernels, fused(): pl.pallas_call(kernel, out_shape=jax.ShapeDtypeStruct((2, 16, 8, 128), F3...  99.5 us

profile of v2, /device:TPU:0, one launch (start us, length us, event | category | flops | bytes accessed | tf_op | source)
XLA Modules:
  0.0 101.1 jit_solution(9443886232820156304)
XLA Ops:
  0.0 99.5 %shard_map.46 = f32[2,16,8,128]{3,2,1,0:T(8,128)} custom-call(s32[8]{0:T(128)} %order_ref.1, f32[2,4,32,3072]{3,2,1,0:T(8,128)} %a_hbm.1, f32[256,3072]{1,0:T(8,128)} %b_hbm.1, f32[1,3072]{1,0:T(1,128)} %bitcast.1), custom_call_target="tpu_custom_call" | custom-call | flops 4831838208 | bytes 12582912 | tf_op jit(solution)/shard_map/pallas_call | solution.py:318
  99.5 1.6 %copy.6 = f32[2,16,8,128]{3,2,1,0:T(8,128)} copy(f32[2,16,8,128]{3,2,1,0:T(8,128)} %shard_map.46) | data formatting | bytes 262144

commit v3 on v2

--- a/solution.py
+++ b/solution.py
@@ -12,7 +12,7 @@
 BF16 = jnp.bfloat16
 SLABS = 8
 CHUNKS = 8
-DEPTH = 3
+DEPTH = 8
 OWN, REM = 0, 1
 
 

time: 101 us -> 101 us (level)
  no operation moved by 1% of the time
where the time goes in v3:
time: 101 us
  Pallas kernels  99.5 us (99%)
  local copies, waits for them, and re-layouts  1.57 us (2%)
    pallas_call x1, Pallas kernels, fused(): pl.pallas_call(kernel, out_shape=jax.ShapeDtypeStruct((2, 16, 8, 128), F3...  99.5 us

profile of v3, /device:TPU:0, one launch (start us, length us, event | category | flops | bytes accessed | tf_op | source)
XLA Modules:
  0.0 101.1 jit_solution(17356403369850187399)
XLA Ops:
  0.0 99.5 %shard_map.46 = f32[2,16,8,128]{3,2,1,0:T(8,128)} custom-call(s32[8]{0:T(128)} %order_ref.1, f32[2,4,32,3072]{3,2,1,0:T(8,128)} %a_hbm.1, f32[256,3072]{1,0:T(8,128)} %b_hbm.1, f32[1,3072]{1,0:T(1,128)} %bitcast.1), custom_call_target="tpu_custom_call" | custom-call | flops 4831838208 | bytes 12582912 | tf_op jit(solution)/shard_map/pallas_call | solution.py:318
  99.5 1.6 %copy.6 = f32[2,16,8,128]{3,2,1,0:T(8,128)} copy(f32[2,16,8,128]{3,2,1,0:T(8,128)} %shard_map.46) | data formatting | bytes 262144

commit v4 on v3

--- a/solution.py
+++ b/solution.py
@@ -12,7 +12,11 @@
 BF16 = jnp.bfloat16
 SLABS = 8
 CHUNKS = 8
-DEPTH = 8
+TWELFTHS = 12
+A_SENT = tuple((t, 0, 12) for t in range(7)) + ((7, 0, 6), (7, 6, 3), (7, 9, 2), (7, 11, 1))
+B_SENT = tuple((32 * t, 32, 0, 12) for t in range(4)) + (
+    (128, 128, 0, 3), (128, 128, 3, 3), (128, 128, 6, 3), (128, 128, 9, 2), (128, 128, 11, 1)
+)
 OWN, REM = 0, 1
 
 
@@ -81,15 +85,15 @@
 
 
 PIECES = {
-    OWN: ((0, 2, 0, 4), (2, 1, 0, 4), (3, 1, 0, 4)),
-    REM: ((0, 3, 0, 2), (0, 3, 2, 1), (0, 3, 3, 1), (3, 1, 0, 4)),
+    OWN: ((0, 2, 0, 8), (2, 1, 0, 8), (3, 1, 0, 8)),
+    REM: ((0, 3, 0, 4), (0, 3, 4, 2), (0, 3, 6, 1), (0, 3, 7, 1), (3, 1, 0, 8)),
 }
 
 
 def kernel(
     order_ref, a_hbm, b_hbm, w_ref, out_ref,
     a_own, b_own, a_rem, b_rem, a_hi, a_lo, b_hi, b_lo, part, sibling, chip, parts, red, plane, picked,
-    gathered,
+    gathered, last_panel, last_rows,
     load_sem, a_send, a_recv, b_send, b_recv, s_send, s_recv, r_send, r_recv, p_send, p_recv, g_send,
     g_recv,
 ):
@@ -120,23 +124,32 @@
         load.start()
     pl.semaphore_wait(barrier, 3 + SLABS - 1)
 
-    def a_copy(t):
+    unit = a_hbm.shape[3] // TWELFTHS
+
+    def span(first, count):
+        return pl.ds(first * unit, count * unit)
+
+    def a_copy(i):
+        t, first, count = A_SENT[i]
         return pltpu.make_async_remote_copy(
-            src_ref=a_chunk(t), dst_ref=a_rem.at[t],
-            send_sem=a_send.at[t], recv_sem=a_recv.at[t],
+            src_ref=a_chunk(t).at[:, :, span(first, count)],
+            dst_ref=a_rem.at[t, :, :, span(first, count)],
+            send_sem=a_send.at[i], recv_sem=a_recv.at[i],
             device_id={"phase": x_near, "slab": d}, device_id_type=MESH,
         )
 
-    def b_copy(t):
+    def b_copy(i):
+        row, rows, first, count = B_SENT[i]
         return pltpu.make_async_remote_copy(
-            src_ref=b_hbm.at[pl.ds(32 * t, 32)], dst_ref=b_rem.at[pl.ds(32 * t, 32)],
-            send_sem=b_send.at[t], recv_sem=b_recv.at[t],
+            src_ref=b_hbm.at[pl.ds(row, rows), span(first, count)],
+            dst_ref=b_rem.at[pl.ds(row, rows), span(first, count)],
+            send_sem=b_send.at[i], recv_sem=b_recv.at[i],
             device_id={"phase": y_near, "slab": d}, device_id_type=MESH,
         )
 
     def core_copy(kind, i):
-        slot, slots, group, groups = PIECES[kind][i]
-        where = (slice(None), pl.ds(slot, slots), pl.ds(group, groups))
+        slot, slots, chunk, chunks = PIECES[kind][i]
+        where = (slice(None), pl.ds(slot, slots), pl.ds(chunk, chunks))
         return pltpu.make_async_remote_copy(
             src_ref=part.at[(kind, 1 - core) + where], dst_ref=sibling.at[(kind,) + where],
             send_sem=s_send.at[kind, i], recv_sem=s_recv.at[kind, i],
@@ -144,9 +157,9 @@
         )
 
     def peer_copy(kind, i, h, act):
-        slot, slots, group, groups = PIECES[kind][i]
+        slot, slots, chunk, chunks = PIECES[kind][i]
         peer_z = ((kind + x) % 2) * 2 + h
-        where = (pl.ds(slot, slots), pl.ds(group, groups))
+        where = (pl.ds(slot, slots), pl.ds(chunk, chunks))
 
         @pl.when(peer_z != z)
         def _():
@@ -158,84 +171,114 @@
 
     def forward(kind, i):
         core_copy(kind, i).wait()
-        slot, slots, group, groups = PIECES[kind][i]
+        slot, slots, chunk, chunks = PIECES[kind][i]
         for h in range(2):
-            where = (h, pl.ds(slot, slots), pl.ds(group, groups))
+            where = (h, pl.ds(slot, slots), pl.ds(chunk, chunks))
             chip[(kind,) + where] = part[(kind, core) + where] + sibling[(kind,) + where]
             peer_copy(kind, i, h, lambda copy: copy.start())
 
-    def split_a(source, t, kind):
-        high, low = split(source[t].reshape(32, -1))
+    def split_a(source, kind, t, first, count):
+        high, low = split(source[t, :, :, span(first, count)].reshape(32, count * unit))
         rows = pl.ds(kind * 256 + 32 * t, 32)
-        a_hi[rows], a_lo[rows] = high, low
-
-    def split_b(source, t, kind):
-        high, low = split(source[pl.ds(32 * t, 32)] * w_ref[...])
-        rows = pl.ds(kind * 256 + 32 * t, 32)
-        b_hi[rows], b_lo[rows] = high, low
-
-    def block(kind, i):
-        slot, slots, group, groups = PIECES[kind][i]
-        rows = pl.ds(kind * 256 + 64 * group, 64 * groups)
-        cols = pl.ds(128 * slot, 128 * slots)
-        value = product(a_hi[rows], a_lo[rows], b_hi[cols], b_lo[cols])
-        value = value.reshape(groups, 2, 4, 8, 128 * slots)
+        a_hi[rows, span(first, count)], a_lo[rows, span(first, count)] = high, low
+
+    def split_b(source, kind, row, count_rows, first, count):
+        cut = span(first, count)
+        for r in range(row, row + count_rows, 32):
+            high, low = split(source[pl.ds(r, 32), cut] * w_ref[:, cut])
+            rows = pl.ds(kind * 256 + r, 32)
+            b_hi[rows, cut], b_lo[rows, cut] = high, low
+
+    def forces(row, rows, col, cols, first=0, count=TWELFTHS):
+        a_at, b_at, cut = pl.ds(row, rows), pl.ds(col, cols), span(first, count)
+        return product(a_hi[a_at, cut], a_lo[a_at, cut], b_hi[b_at, cut], b_lo[b_at, cut])
+
+    def put(kind, i, value):
+        slot, slots, chunk, chunks = PIECES[kind][i]
+        value = value.reshape(chunks, 4, 8, 128 * slots)
         for kk in range(4):
             for s in range(slots):
-                part[kind, kk % 2, kk // 2, slot + s, pl.ds(group, groups)] = (
-                    value[:, :, kk, :, 128 * s:128 * (s + 1)]
+                part[kind, kk % 2, kk // 2, slot + s, pl.ds(chunk, chunks)] = (
+                    value[:, kk, :, 128 * s:128 * (s + 1)]
                 )
         core_copy(kind, i).start()
 
-    for t in range(DEPTH):
-        a_copy(t).start()
-        b_copy(t).start()
+    def block(kind, i):
+        slot, slots, chunk, chunks = PIECES[kind][i]
+        put(kind, i, forces(kind * 256 + 32 * chunk, 32 * chunks, 128 * slot, 128 * slots))
+
+    def take_a(i):
+        a_copy(i).wait()
+        split_a(a_rem, REM, *A_SENT[i])
+
+    def take_b(i):
+        b_copy(i).wait()
+        split_b(b_rem, REM, *B_SENT[i])
+
+    for i in range(max(len(A_SENT), len(B_SENT))):
+        if i < len(A_SENT):
+            a_copy(i).start()
+        if i < len(B_SENT):
+            b_copy(i).start()
 
     for load in loads:
         load.wait()
     for t in range(CHUNKS):
-        split_a(a_own, t, OWN)
-        split_b(b_own, t, OWN)
+        split_a(a_own, OWN, t, 0, TWELFTHS)
+        split_b(b_own, OWN, 32 * t, 32, 0, TWELFTHS)
     block(OWN, 0)
 
-    for t in range(CHUNKS):
-        b_copy(t).wait()
-        if t + DEPTH < CHUNKS:
-            b_copy(t + DEPTH).start()
-        split_b(b_rem, t, REM)
-        if t == 7:
-            block(OWN, 2)
-        a_copy(t).wait()
-        if t + DEPTH < CHUNKS:
-            a_copy(t + DEPTH).start()
-        split_a(a_rem, t, REM)
-        if t == 0:
+    for i in range(4):
+        take_a(i)
+        take_b(i)
+        if i == 0:
             forward(OWN, 0)
-        if t == 3:
-            block(REM, 0)
-            block(OWN, 1)
-        if t == 4:
-            forward(REM, 0)
-            forward(OWN, 1)
-        if t == 5:
-            block(REM, 1)
-        if t == 6:
-            forward(REM, 1)
-        if t == 7:
-            block(REM, 3)
-            forward(OWN, 2)
-            block(REM, 2)
-            forward(REM, 3)
-            forward(REM, 2)
+    block(REM, 0)
+    block(OWN, 1)
+    take_a(4)
+    take_b(4)
+    forward(REM, 0)
+    forward(OWN, 1)
+    take_a(5)
+    take_b(5)
+    block(REM, 1)
+    take_a(6)
+    take_b(6)
+    forward(REM, 1)
+    block(REM, 2)
+    last_panel[pl.ds(0, 480)] = forces(0, 480, 384, 128, 0, 9)
+    take_a(7)
+    forward(REM, 2)
+    value = forces(480, 32, 0, 512, 0, 6)
+    last_rows[...] = value[:, :384]
+    last_panel[pl.ds(480, 32)] = value[:, 384:]
+    take_b(7)
+    last_panel[pl.ds(0, 480)] += forces(0, 480, 384, 128, 9, 2)
+    take_a(8)
+    value = forces(480, 32, 0, 512, 6, 3)
+    last_rows[...] += value[:, :384]
+    last_panel[pl.ds(480, 32)] += value[:, 384:]
+    take_a(9)
+    value = forces(480, 32, 0, 512, 9, 2)
+    last_rows[...] += value[:, :384]
+    last_panel[pl.ds(480, 32)] += value[:, 384:]
+    take_b(8)
+    put(OWN, 2, last_panel[pl.ds(0, 256)] + forces(0, 256, 384, 128, 11, 1))
+    take_a(10)
+    put(REM, 4, last_panel[pl.ds(256, 256)] + forces(256, 256, 384, 128, 11, 1))
+    put(REM, 3, last_rows[...] + forces(480, 32, 0, 384, 11, 1))
+    forward(OWN, 2)
+    forward(REM, 4)
+    forward(REM, 3)
 
     mine = (d // 4 + x) % 2
     for kind in (OWN, REM):
         @pl.when(mine == kind)
         def _():
-            for i, (slot, slots, group, groups) in enumerate(PIECES[kind]):
+            for i, (slot, slots, chunk, chunks) in enumerate(PIECES[kind]):
                 for o in range(1, 4):
                     other = (z + o) % 4
-                    landed = parts.at[other, pl.ds(slot, slots), pl.ds(group, groups)]
+                    landed = parts.at[other, pl.ds(slot, slots), pl.ds(chunk, chunks)]
                     pltpu.make_async_copy(landed, landed, r_recv.at[i, other]).wait()
 
     total = chip[mine, z % 2]
@@ -246,14 +289,14 @@
     def plane_copy(o):
         peer = (p + o) % 4
         return pltpu.make_async_remote_copy(
-            src_ref=red.at[:, peer], dst_ref=plane.at[pl.ds(4 * p, 4)],
+            src_ref=red.at[:, pl.ds(2 * peer, 2)], dst_ref=plane.at[pl.ds(4 * p, 4)],
             send_sem=p_send.at[o], recv_sem=p_recv.at[p],
             device_id={"phase": peer, "slab": d}, device_id_type=MESH,
         )
 
     for o in range(1, 4):
         plane_copy(o).start()
-    plane[pl.ds(4 * p, 4)] = red[:, p]
+    plane[pl.ds(4 * p, 4)] = red[:, pl.ds(2 * p, 2)]
     for o in range(1, 4):
         other = (p + o) % 4
         landed = plane.at[pl.ds(4 * other, 4)]
@@ -334,18 +377,20 @@
             vmem((512, points), BF16),
             vmem((512, points), BF16),
             vmem((512, points), BF16),
-            vmem((2, 2, 2, 4, 4, 2, 8, 128), F32),
-            vmem((2, 2, 4, 4, 2, 8, 128), F32),
-            vmem((2, 2, 4, 4, 2, 8, 128), F32),
-            vmem((4, 4, 4, 2, 8, 128), F32),
-            vmem((4, 4, 2, 8, 128), F32),
+            vmem((2, 2, 2, 4, CHUNKS, 8, 128), F32),
+            vmem((2, 2, 4, CHUNKS, 8, 128), F32),
+            vmem((2, 2, 4, CHUNKS, 8, 128), F32),
+            vmem((4, 4, CHUNKS, 8, 128), F32),
+            vmem((4, CHUNKS, 8, 128), F32),
             vmem((16, 2, 8, 128), F32),
             vmem((8, 2, 2, 8, 128), F32),
             vmem((8, 2, 2, 8, 128), F32),
+            vmem((512, 128), F32),
+            vmem((32, 384), F32),
             dma((CHUNKS + 1,)),
-            dma((CHUNKS,)), dma((CHUNKS,)), dma((CHUNKS,)), dma((CHUNKS,)),
-            dma((2, 4)), dma((2, 4)),
-            dma((2, 4, 2)), dma((4, 4)),
+            dma((len(A_SENT),)), dma((len(A_SENT),)), dma((len(B_SENT),)), dma((len(B_SENT),)),
+            dma((2, 5)), dma((2, 5)),
+            dma((2, 5, 2)), dma((5, 4)),
             dma((4,)), dma((4,)),
             dma((8,)), dma((8,)),
         ],
@@ -364,7 +409,7 @@
             mesh.shape["phase"] == 4
             and mesh.shape["slab"] == SLABS
             and pressure.shape[:3] == (2, 4, 32)
-            and pressure.shape[3] % 256 == 0
+            and pressure.shape[3] % 1536 == 0
             and pressure.shape[3] <= 3072
             and mode_shapes.shape[0] == 256
             and panel_order.shape[0] == 8

time: 101 us -> 99.6 us (0.986)
  Pallas kernels: 99.5 us -> 97.8 us
    pallas_call x1, Pallas kernels: 99.5 us -> 97.8 us  [fused(): pl.pallas_call(kernel, out_shape=jax.ShapeDtypeStruct((2, 16, 8, 128), F3...]
where the time goes in v4:
time: 99.6 us; the launch traced here: 99.4 us
  Pallas kernels  97.8 us (98%)
  local copies, waits for them, and re-layouts  1.57 us (2%)
    pallas_call x1, Pallas kernels, fused(): pl.pallas_call(kernel, out_shape=jax.ShapeDtypeStruct((2, 16, 8, 128), F3...  97.8 us

profile of v4, /device:TPU:0, one launch (start us, length us, event | category | flops | bytes accessed | tf_op | source)
XLA Modules:
  0.0 99.4 jit_solution(16320553812418411064)
XLA Ops:
  0.0 97.8 %shard_map.46 = f32[2,16,8,128]{3,2,1,0:T(8,128)} custom-call(s32[8]{0:T(128)} %order_ref.1, f32[2,4,32,3072]{3,2,1,0:T(8,128)} %a_hbm.1, f32[256,3072]{1,0:T(8,128)} %b_hbm.1, f32[1,3072]{1,0:T(1,128)} %bitcast.1), custom_call_target="tpu_custom_call" | custom-call | flops 4831838208 | bytes 12582912 | tf_op jit(solution)/shard_map/pallas_call | solution.py:361
  97.8 1.6 %copy.6 = f32[2,16,8,128]{3,2,1,0:T(8,128)} copy(f32[2,16,8,128]{3,2,1,0:T(8,128)} %shard_map.46) | data formatting | bytes 262144

commit v5 on v4

--- a/solution.py
+++ b/solution.py
@@ -14,8 +14,8 @@
 CHUNKS = 8
 TWELFTHS = 12
 A_SENT = tuple((t, 0, 12) for t in range(7)) + ((7, 0, 6), (7, 6, 3), (7, 9, 2), (7, 11, 1))
-B_SENT = tuple((32 * t, 32, 0, 12) for t in range(4)) + (
-    (128, 128, 0, 3), (128, 128, 3, 3), (128, 128, 6, 3), (128, 128, 9, 2), (128, 128, 11, 1)
+B_SENT = tuple((32 * t, 32, 0, 12) for t in range(7)) + (
+    (224, 32, 0, 6), (224, 32, 6, 3), (224, 32, 9, 2), (224, 32, 11, 1)
 )
 OWN, REM = 0, 1
 
@@ -85,15 +85,15 @@
 
 
 PIECES = {
-    OWN: ((0, 2, 0, 8), (2, 1, 0, 8), (3, 1, 0, 8)),
-    REM: ((0, 3, 0, 4), (0, 3, 4, 2), (0, 3, 6, 1), (0, 3, 7, 1), (3, 1, 0, 8)),
+    OWN: ((0, 2, 0, 8), (2, 1, 0, 8), (3, 1, 0, 8), (4, 1, 0, 2)),
+    REM: ((0, 3, 0, 4), (0, 3, 4, 2), (0, 3, 6, 1), (3, 1, 0, 7), (4, 1, 0, 2), (0, 4, 7, 1)),
 }
 
 
 def kernel(
     order_ref, a_hbm, b_hbm, w_ref, out_ref,
     a_own, b_own, a_rem, b_rem, a_hi, a_lo, b_hi, b_lo, part, sibling, chip, parts, red, plane, picked,
-    gathered, last_panel, last_rows,
+    gathered, last_cols, last_rows,
     load_sem, a_send, a_recv, b_send, b_recv, s_send, s_recv, r_send, r_recv, p_send, p_recv, g_send,
     g_recv,
 ):
@@ -246,30 +246,50 @@
     take_b(6)
     forward(REM, 1)
     block(REM, 2)
-    last_panel[pl.ds(0, 480)] = forces(0, 480, 384, 128, 0, 9)
+    lane = lax.broadcasted_iota(jnp.int32, (4, 8, 128), 2)
+    value = forces(0, 480, 384, 128)
+    value = jnp.where(lax.broadcasted_iota(jnp.int32, (480, 128), 1) < 96, value, 0.0)
+    put(OWN, 2, value[:256])
+    put(REM, 3, value[256:])
+
+    def late(first, count):
+        return forces(0, 480, 384, 128, first, count), forces(480, 32, 0, 512, first, count)
+
     take_a(7)
+    take_b(7)
+    last_cols[...], last_rows[...] = late(0, 6)
     forward(REM, 2)
-    value = forces(480, 32, 0, 512, 0, 6)
-    last_rows[...] = value[:, :384]
-    last_panel[pl.ds(480, 32)] = value[:, 384:]
-    take_b(7)
-    last_panel[pl.ds(0, 480)] += forces(0, 480, 384, 128, 9, 2)
-    take_a(8)
-    value = forces(480, 32, 0, 512, 6, 3)
-    last_rows[...] += value[:, :384]
-    last_panel[pl.ds(480, 32)] += value[:, 384:]
-    take_a(9)
-    value = forces(480, 32, 0, 512, 9, 2)
-    last_rows[...] += value[:, :384]
-    last_panel[pl.ds(480, 32)] += value[:, 384:]
-    take_b(8)
-    put(OWN, 2, last_panel[pl.ds(0, 256)] + forces(0, 256, 384, 128, 11, 1))
+    forward(OWN, 2)
+    forward(REM, 3)
+    for i, first, count in ((8, 6, 3), (9, 9, 2)):
+        take_a(i)
+        take_b(i)
+        cols, rows = late(first, count)
+        last_cols[...] += cols
+        last_rows[...] += rows
     take_a(10)
-    put(REM, 4, last_panel[pl.ds(256, 256)] + forces(256, 256, 384, 128, 11, 1))
-    put(REM, 3, last_rows[...] + forces(480, 32, 0, 384, 11, 1))
-    forward(OWN, 2)
+    take_b(10)
+    cols, rows = late(11, 1)
+    put(REM, 5, last_rows[...] + rows)
+    cols = last_cols[...] + cols
+    for kind in (REM, OWN):
+        for c in range(2):
+            packed = jnp.zeros((4, 8, 128), F32)
+            for g in range(4):
+                at = kind * 256 + 32 * (2 * g + c)
+                if at >= 480:
+                    continue
+                moved = cols[at:at + 32].reshape(4, 8, 128)
+                if g < 3:
+                    moved = pltpu.roll(moved, 32 * (g + 1), 2)
+                inside = jnp.logical_and(lane >= 32 * g, lane < 32 * (g + 1))
+                packed = jnp.where(inside, moved, packed)
+            for kk in range(4):
+                part[kind, kk % 2, kk // 2, 4, c] = packed[kk]
+        core_copy(kind, 4 if kind == REM else 3).start()
+    forward(REM, 5)
     forward(REM, 4)
-    forward(REM, 3)
+    forward(OWN, 3)
 
     mine = (d // 4 + x) % 2
     for kind in (OWN, REM):
@@ -284,7 +304,13 @@
     total = chip[mine, z % 2]
     for o in range(1, 4):
         total = total + parts[(z + o) % 4]
-    red[...] = total
+    red[...] = total[:4]
+    for c in range(2):
+        for g in range(4):
+            moved = total[4, c]
+            if g < 3:
+                moved = pltpu.roll(moved, 96 - 32 * g, 1)
+            red[3, 2 * g + c] = total[3, 2 * g + c] + jnp.where(lane[0] >= 96, moved, 0.0)
 
     def plane_copy(o):
         peer = (p + o) % 4
@@ -377,20 +403,20 @@
             vmem((512, points), BF16),
             vmem((512, points), BF16),
             vmem((512, points), BF16),
-            vmem((2, 2, 2, 4, CHUNKS, 8, 128), F32),
-            vmem((2, 2, 4, CHUNKS, 8, 128), F32),
-            vmem((2, 2, 4, CHUNKS, 8, 128), F32),
-            vmem((4, 4, CHUNKS, 8, 128), F32),
+            vmem((2, 2, 2, 5, CHUNKS, 8, 128), F32),
+            vmem((2, 2, 5, CHUNKS, 8, 128), F32),
+            vmem((2, 2, 5, CHUNKS, 8, 128), F32),
+            vmem((4, 5, CHUNKS, 8, 128), F32),
             vmem((4, CHUNKS, 8, 128), F32),
             vmem((16, 2, 8, 128), F32),
             vmem((8, 2, 2, 8, 128), F32),
             vmem((8, 2, 2, 8, 128), F32),
-            vmem((512, 128), F32),
-            vmem((32, 384), F32),
+            vmem((480, 128), F32),
+            vmem((32, 512), F32),
             dma((CHUNKS + 1,)),
             dma((len(A_SENT),)), dma((len(A_SENT),)), dma((len(B_SENT),)), dma((len(B_SENT),)),
-            dma((2, 5)), dma((2, 5)),
-            dma((2, 5, 2)), dma((5, 4)),
+            dma((2, 6)), dma((2, 6)),
+            dma((2, 6, 2)), dma((6, 4)),
             dma((4,)), dma((4,)),
             dma((8,)), dma((8,)),
         ],

time: 99.6 us -> 99.8 us (level)
  no operation moved by 1% of the time
where the time goes in v5:
time: 99.8 us; the launch traced here: 99.5 us
  Pallas kernels  97.9 us (98%)
  local copies, waits for them, and re-layouts  1.57 us (2%)
    pallas_call x1, Pallas kernels, fused(): pl.pallas_call(kernel, out_shape=jax.ShapeDtypeStruct((2, 16, 8, 128), F3...  97.9 us

profile of v5, /device:TPU:0, one launch (start us, length us, event | category | flops | bytes accessed | tf_op | source)
XLA Modules:
  0.0 99.5 jit_solution(8661073076934339959)
XLA Ops:
  0.0 97.9 %shard_map.46 = f32[2,16,8,128]{3,2,1,0:T(8,128)} custom-call(s32[8]{0:T(128)} %order_ref.1, f32[2,4,32,3072]{3,2,1,0:T(8,128)} %a_hbm.1, f32[256,3072]{1,0:T(8,128)} %b_hbm.1, f32[1,3072]{1,0:T(1,128)} %bitcast.1), custom_call_target="tpu_custom_call" | custom-call | flops 4831838208 | bytes 12582912 | tf_op jit(solution)/shard_map/pallas_call | solution.py:387
  98.0 1.6 %copy.6 = f32[2,16,8,128]{3,2,1,0:T(8,128)} copy(f32[2,16,8,128]{3,2,1,0:T(8,128)} %shard_map.46) | data formatting | bytes 262144

commit v6 on v4

--- a/solution.py
+++ b/solution.py
@@ -91,9 +91,9 @@
 
 
 def kernel(
-    order_ref, a_hbm, b_hbm, w_ref, out_ref,
+    order_ref, a_hbm, b_hbm, w_ref, gathered,
     a_own, b_own, a_rem, b_rem, a_hi, a_lo, b_hi, b_lo, part, sibling, chip, parts, red, plane, picked,
-    gathered, last_panel, last_rows,
+    last_panel, last_rows,
     load_sem, a_send, a_recv, b_send, b_recv, s_send, s_recv, r_send, r_recv, p_send, p_recv, g_send,
     g_recv,
 ):
@@ -326,6 +326,17 @@
         landed = gathered.at[other]
         pltpu.make_async_copy(landed, landed, g_recv.at[other]).wait()
 
+    for kind in (OWN, REM):
+        for i in range(len(PIECES[kind])):
+            for h in range(2):
+                peer_copy(kind, i, h, lambda copy: copy.wait_send())
+    for o in range(1, 4):
+        plane_copy(o).wait_send()
+    for o in range(1, SLABS):
+        slab_copy(o).wait_send()
+
+
+def blade_kernel(gathered, out_ref):
     blades = 16
     scale = 1.0 / math.sqrt(blades)
     cosine = [round(math.cos(2 * math.pi * i / blades), 15) * scale for i in range(blades)]
@@ -344,23 +355,14 @@
         out_ref[0, b] = real
         out_ref[1, b] = imag
 
-    for kind in (OWN, REM):
-        for i in range(len(PIECES[kind])):
-            for h in range(2):
-                peer_copy(kind, i, h, lambda copy: copy.wait_send())
-    for o in range(1, 4):
-        plane_copy(o).wait_send()
-    for o in range(1, SLABS):
-        slab_copy(o).wait_send()
-
 
 def fused(pressure, mode_shapes, point_weight, panel_order):
     points = pressure.shape[3]
     vmem = pltpu.VMEM
     dma = pltpu.SemaphoreType.DMA
-    return pl.pallas_call(
+    gathered = pl.pallas_call(
         kernel,
-        out_shape=jax.ShapeDtypeStruct((2, 16, 8, 128), F32),
+        out_shape=jax.ShapeDtypeStruct((8, 2, 2, 8, 128), F32),
         in_specs=[
             pl.BlockSpec(memory_space=pltpu.SMEM),
             pl.BlockSpec(memory_space=pl.ANY),
@@ -384,7 +386,6 @@
             vmem((4, CHUNKS, 8, 128), F32),
             vmem((16, 2, 8, 128), F32),
             vmem((8, 2, 2, 8, 128), F32),
-            vmem((8, 2, 2, 8, 128), F32),
             vmem((512, 128), F32),
             vmem((32, 384), F32),
             dma((CHUNKS + 1,)),
@@ -401,6 +402,9 @@
             flops=6 * 512 * 512 * points, bytes_accessed=16 * 256 * points, transcendentals=0
         ),
     )(panel_order, pressure, mode_shapes, point_weight.reshape(1, points))
+    return pl.pallas_call(
+        blade_kernel, out_shape=jax.ShapeDtypeStruct((2, 16, 8, 128), F32),
+    )(gathered)
 
 
 def solution(mesh):

time: 99.6 us -> 99.6 us (level)
  Pallas kernels: 97.8 us -> 99.4 us
  local copies, waits for them, and re-layouts: 1.57 us -> 0 us
    pallas_call x1 -> x2, Pallas kernels: 97.8 us -> 99.4 us  [the longest x1 97.6 us: fused(): pl.pallas_call(kernel, out_shape=jax.ShapeDtypeStruct((8, 2, 2, 8, 128),...]
    unnamed x1 -> x0, local copies, waits for them, and re-layouts: 1.57 us -> none
where the time goes in v6:
time: 99.6 us; the launch traced here: 99.4 us
  Pallas kernels  99.4 us (100%)
    pallas_call x1, Pallas kernels, fused(): pl.pallas_call(kernel, out_shape=jax.ShapeDtypeStruct((8, 2, 2, 8, 128),...  97.6 us

profile of v6, /device:TPU:0, one launch (start us, length us, event | category | flops | bytes accessed | tf_op | source)
XLA Modules:
  0.0 99.4 jit_solution(5994005053714203170)
XLA Ops:
  0.0 97.6 %shard_map.46.gathered = f32[8,2,2,8,128]{4,3,2,1,0:T(8,128)} custom-call(s32[8]{0:T(128)} %order_ref.1, f32[2,4,32,3072]{3,2,1,0:T(8,128)} %a_hbm.1, f32[256,3072]{1,0:T(8,128)} %b_hbm.1, f32[1,3072]{1,0:T(1,128)} %bitcast.1), custom_call_target="tpu_custom_call" | custom-call | flops 4831838208 | bytes 12582912 | tf_op jit(solution)/shard_map/pallas_call | solution.py:363
  97.6 1.8 %shard_map.47 = f32[2,16,8,128]{3,2,1,0:T(8,128)} custom-call(f32[8,2,2,8,128]{4,3,2,1,0:T(8,128)} %shard_map.46.gathered), custom_call_target="tpu_custom_call" | custom-call | tf_op jit(solution)/shard_map/pallas_call | solution.py:405
